TPU v7x, 512 devices: a whole 4x4x16 slice. The times are simulated.
512 devices in a mesh: dp: 32 (over z, core), blk: 16 (over y, x).
Axes of the slice: x: 4, y: 4, z: 16, core: 2. Of those that a mesh axis runs over, the one named last changes fastest.
Arguments:
- partials: bfloat16 [32, 2048, 7168], P('dp', 'blk'), may hold values from -256 to 256
- counts: int32 [32], P('dp'), may hold values from 8 to 32
Outputs:
- update: float32 [2048, 7168], P('blk', 'dp')
All inputs are finite; a program needn't handle non-finite values.
Results may differ from a plain program's by a relative error of at most 0.0003.
Values sent between devices are 32-bit elements; how exact they have to be, the bound alone decides.
A program may use at most 64 MiB of HBM per device.

v0:
```python
import math

import jax
import jax.numpy as jnp
from jax import lax
from jax.sharding import PartitionSpec as P

H = 2048
D = 7168
ITERS = 3


COEF_A = 3.4445
COEF_B = -4.775
COEF_C = 2.0315
EPS = 1e-07


def mult(left, right):
    return jnp.dot(left, right, precision=lax.Precision.HIGHEST, preferred_element_type=jnp.float32)


def mult_t(left, right):
    return lax.dot_general(
        left,
        right,
        (((1,), (1,)), ((), ())),
        precision=lax.Precision.HIGHEST,
        preferred_element_type=jnp.float32,
    )


def products(field):
    whole = lax.all_gather(field, "blk", axis=0, tiled=True)
    gram_part = mult_t(field, whole)
    gram = lax.psum(gram_part, "dp")
    prod = mult(gram, whole)
    prod_whole = lax.all_gather(prod, "blk", axis=0, tiled=True)
    second = mult(gram, prod_whole)
    return (gram, prod, second)


def body(partials, counts):
    weight = counts[0].astype(jnp.float32)
    weighted = partials[0].astype(jnp.float32) * weight
    field = lax.psum_scatter(weighted, "dp", scatter_dimension=1, tiled=True)
    total_sq = lax.psum(jnp.sum(field * field), ("dp", "blk"))
    field = field / (jnp.sqrt(total_sq) + EPS)
    for turn in range(ITERS):
        gram, prod, second = products(field)
        field = COEF_A * field + COEF_B * prod + COEF_C * second
    return 0.2 * math.sqrt(max(H, D)) * field


def solution(mesh):
    placed = (P("dp", "blk", None), P("dp"))
    return jax.shard_map(
        body, mesh=mesh, in_specs=placed, out_specs=P("blk", "dp"), check_vma=False
    )
```

profile of v0, /device:TPU:1, one launch (start us, length us, event | category | flops | bytes accessed | tf_op | source)
XLA Modules:
  0.0 1272.2 jit_solution(14638536181001339620)
XLA Ops:
  7.2 3.3 copy.3
  10.5 2.0 multiply_bitcast_fusion
  12.6 114.8 %reduce-scatter.2.cloned.1.call-done = f32[128,224]{0,1:T(8,128)} async-done(((f32[128,7168]{0,1:T(8,128)}), f32[128,224]{0,1:T(8,128)}) %reduce-scatter.2.cloned.1.call-update) | async-done | bytes 114704 | tf_op jit(solution)/shard_map/reduce_scatter | solution.py:46
  127.4 1.5 multiply_reduce_fusion
  128.9 106.5 %psum.28 = f32[]{:T(128)} all-reduce(f32[]{:T(128)} %multiply_reduce_fusion), channel_id=1, replica_groups=mesh['dp'=32,'blk'=16] {'dp','blk'}, use_global_device_ids=true, to_apply=%region_2.0 | all-reduce | flops 1 | bytes 8 | tf_op jit(solution)/shard_map/psum | solution.py:47
  236.1 1.6 broadcast_divide_fusion
  237.8 55.8 %all-gather.7.cloned.1.call-done = f32[2048,224]{0,1:T(8,128)} async-done(((f32[128,224]{0,1:T(8,128)}), f32[2048,224]{0,1:T(8,128)}) %all-gather.7.cloned.1.call-update) | async-done | bytes 1835024 | tf_op jit(solution)/shard_map/all_gather | solution.py:34
  293.5 3.8 fusion.4
  297.4 211.0 %all-reduce.4.cloned.1.call-done = f32[128,2048]{1,0:T(8,128)} async-done(((f32[128,2048]{1,0:T(8,128)}), f32[128,2048]{1,0:T(8,128)}) %all-reduce.4.cloned.1.call-update) | async-done | bytes 1048592 | tf_op jit(solution)/shard_map/psum | solution.py:36
  508.4 3.6 fusion.5
  512.1 60.7 %all-gather.9.cloned.1.call-done = f32[2048,224]{0,1:T(8,128)} async-done(((f32[128,224]{0,1:T(8,128)}), f32[2048,224]{0,1:T(8,128)}) %all-gather.9.cloned.1.call-update) | async-done | bytes 1835024 | tf_op jit(solution)/shard_map/all_gather | solution.py:38
  572.8 3.7 fusion.2
  576.6 61.4 %all-gather.11.cloned.1.call-done = f32[2048,224]{0,1:T(8,128)} async-done(((f32[128,224]{0,1:T(8,128)}), f32[2048,224]{0,1:T(8,128)}) %all-gather.11.cloned.1.call-update) | async-done | bytes 1835024 | tf_op jit(solution)/shard_map/all_gather | solution.py:34
  638.0 3.8 fusion.6
  641.9 211.0 %all-reduce.6.cloned.1.call-done = f32[128,2048]{1,0:T(8,128)} async-done(((f32[128,2048]{1,0:T(8,128)}), f32[128,2048]{1,0:T(8,128)}) %all-reduce.6.cloned.1.call-update) | async-done | bytes 1048592 | tf_op jit(solution)/shard_map/psum | solution.py:36
  852.8 3.6 fusion.7
  856.5 60.7 %all-gather.13.cloned.1.call-done = f32[2048,224]{0,1:T(8,128)} async-done(((f32[128,224]{0,1:T(8,128)}), f32[2048,224]{0,1:T(8,128)}) %all-gather.13.cloned.1.call-update) | async-done | bytes 1835024 | tf_op jit(solution)/shard_map/all_gather | solution.py:38
  917.2 3.7 fusion.1
  921.2 61.2 %all-gather.15.cloned.1.call-done = f32[2048,224]{0,1:T(8,128)} async-done(((f32[128,224]{0,1:T(8,128)}), f32[2048,224]{0,1:T(8,128)}) %all-gather.15.cloned.1.call-update) | async-done | bytes 1835024 | tf_op jit(solution)/shard_map/all_gather | solution.py:34
  982.4 3.8 fusion.8
  986.3 211.0 %all-reduce.8.cloned.1.call-done = f32[128,2048]{1,0:T(8,128)} async-done(((f32[128,2048]{1,0:T(8,128)}), f32[128,2048]{1,0:T(8,128)}) %all-reduce.8.cloned.1.call-update) | async-done | bytes 1048592 | tf_op jit(solution)/shard_map/psum | solution.py:36
  1197.2 3.6 fusion.9
  1200.8 60.7 %all-gather.17.cloned.1.call-done = f32[2048,224]{0,1:T(8,128)} async-done(((f32[128,224]{0,1:T(8,128)}), f32[2048,224]{0,1:T(8,128)}) %all-gather.17.cloned.1.call-update) | async-done | bytes 1835024 | tf_op jit(solution)/shard_map/all_gather | solution.py:38
  1261.6 3.7 fusion.3
  (38 shorter events, 0.8 us)
Async XLA Ops:
  6.5 120.9 %reduce-scatter.2.cloned.1.call-start = ((), (), s32[]{:S(2)}) async-start(), calls=%async_computation.1 | async-start | bytes 3784704 | tf_op jit(solution)/shard_map/reduce_scatter | solution.py:46
  12.5 281.0 %all-gather.7.cloned.1.call-start = ((), (), s32[]{:S(2)}) async-start(), calls=%async_computation.2 | async-start | bytes 1949696 | tf_op jit(solution)/shard_map/all_gather | solution.py:34
  237.7 270.7 %all-reduce.4.cloned.1.call-start = ((), (), s32[]{:S(2)}) async-start(), calls=%async_computation.3 | async-start | bytes 2097152 | tf_op jit(solution)/shard_map/psum | solution.py:36
  293.5 214.9 %copy-start = (f32[2048,224]{0,1:T(8,128)S(1)}, f32[2048,224]{0,1:T(8,128)}, u32[]{:S(2)}) copy-start(f32[2048,224]{0,1:T(8,128)} %all-gather.7.cloned.1.call-done) | copy-start | bytes 5505028
  297.4 275.4 %copy-start.6 = (f32[128,224]{0,1:T(8,128)S(1)}, f32[128,224]{0,1:T(8,128)}, u32[]{:S(2)}) copy-start(f32[128,224]{0,1:T(8,128)} %broadcast_divide_fusion) | copy-start | bytes 344068
  297.4 275.4 %all-gather.9.cloned.1.call-start = ((), (), s32[]{:S(2)}) async-start(), calls=%async_computation.4 | async-start | bytes 1949696 | tf_op jit(solution)/shard_map/all_gather | solution.py:38
  508.4 64.3 %copy-start.3 = (f32[128,2048]{1,0:T(8,128)S(1)}, f32[128,2048]{1,0:T(8,128)}, u32[]{:S(2)}) copy-start(f32[128,2048]{1,0:T(8,128)} %all-reduce.4.cloned.1.call-done) | copy-start | bytes 3145732
  512.0 125.9 %all-gather.11.cloned.1.call-start = ((), (), s32[]{:S(2)}) async-start(), calls=%async_computation.5 | async-start | bytes 1949696 | tf_op jit(solution)/shard_map/all_gather | solution.py:34
  576.5 276.3 %all-reduce.6.cloned.1.call-start = ((), (), s32[]{:S(2)}) async-start(), calls=%async_computation.6 | async-start | bytes 2097152 | tf_op jit(solution)/shard_map/psum | solution.py:36
  637.9 214.9 %copy-start.1 = (f32[2048,224]{0,1:T(8,128)S(1)}, f32[2048,224]{0,1:T(8,128)}, u32[]{:S(2)}) copy-start(f32[2048,224]{0,1:T(8,128)} %all-gather.11.cloned.1.call-done) | copy-start | bytes 5505028
  641.8 275.4 %copy-start.7 = (f32[128,224]{0,1:T(8,128)S(1)}, f32[128,224]{0,1:T(8,128)}, u32[]{:S(2)}) copy-start(f32[128,224]{0,1:T(8,128)} %fusion.2) | copy-start | bytes 344068
  641.8 275.4 %all-gather.13.cloned.1.call-start = ((), (), s32[]{:S(2)}) async-start(), calls=%async_computation.7 | async-start | bytes 1949696 | tf_op jit(solution)/shard_map/all_gather | solution.py:38
  852.8 64.3 %copy-start.4 = (f32[128,2048]{1,0:T(8,128)S(1)}, f32[128,2048]{1,0:T(8,128)}, u32[]{:S(2)}) copy-start(f32[128,2048]{1,0:T(8,128)} %all-reduce.6.cloned.1.call-done) | copy-start | bytes 3145732
  856.4 125.9 %all-gather.15.cloned.1.call-start = ((), (), s32[]{:S(2)}) async-start(), calls=%async_computation.8 | async-start | bytes 1949696 | tf_op jit(solution)/shard_map/all_gather | solution.py:34
  920.9 276.3 %all-reduce.8.cloned.1.call-start = ((), (), s32[]{:S(2)}) async-start(), calls=%async_computation.9 | async-start | bytes 2097152 | tf_op jit(solution)/shard_map/psum | solution.py:36
  982.4 214.9 %copy-start.2 = (f32[2048,224]{0,1:T(8,128)S(1)}, f32[2048,224]{0,1:T(8,128)}, u32[]{:S(2)}) copy-start(f32[2048,224]{0,1:T(8,128)} %all-gather.15.cloned.1.call-done) | copy-start | bytes 5505028
  986.2 275.4 %copy-start.8 = (f32[128,224]{0,1:T(8,128)S(1)}, f32[128,224]{0,1:T(8,128)}, u32[]{:S(2)}) copy-start(f32[128,224]{0,1:T(8,128)} %fusion.1) | copy-start | bytes 344068
  986.2 275.3 %all-gather.17.cloned.1.call-start = ((), (), s32[]{:S(2)}) async-start(), calls=%async_computation.10 | async-start | bytes 1949696 | tf_op jit(solution)/shard_map/all_gather | solution.py:38
  1197.2 64.3 %copy-start.5 = (f32[128,2048]{1,0:T(8,128)S(1)}, f32[128,2048]{1,0:T(8,128)}, u32[]{:S(2)}) copy-start(f32[128,2048]{1,0:T(8,128)} %all-reduce.8.cloned.1.call-done) | copy-start | bytes 3145732
Sparse Core Ops, SparseCore 0:
  12.7 114.6 reduce-scatter.1
  237.8 55.6 all-gather.6
  297.5 210.8 all-reduce.3
  512.2 60.5 all-gather.8
  576.7 61.2 all-gather.10
  641.9 210.8 all-reduce.5
  856.5 60.5 all-gather.12
  921.1 61.2 all-gather.14
  986.3 210.8 all-reduce.7
  1200.9 60.5 all-gather.16
where the time goes:
time: 1270 us
  waiting for transfers between devices  1110 us (87%)
  blocking collectives  107 us (8%)
  matrix products  33.4 us (3%)
  between operations  14.9 us (1%)
    psum x3, waiting for transfers between devices, products(): gram = lax.psum(gram_part, 'dp')  633 us
    all_gather x3, waiting for transfers between devices, products(): prod_whole = lax.all_gather(prod, 'blk', axis=0, tiled=True)  182 us
    all_gather x3, waiting for transfers between devices, products(): whole = lax.all_gather(field, 'blk', axis=0, tiled=True)  178 us
    reduce_scatter x1, waiting for transfers between devices, body(): field = lax.psum_scatter(weighted, 'dp', scatter_dimension=1, tiled=True)  115 us
    psum x1, blocking collectives, body(): total_sq = lax.psum(jnp.sum(field * field), ('dp', 'blk'))  107 us
  transfers between devices with their start and end apart: 10, of which 10 were waited for; matrix products, arithmetic and copies ran while one was open for 0% of the time, Pallas kernels for 0%

commit v1 on v0

v1 whole, which is shorter than its diff:
```python
import math

import jax
import jax.numpy as jnp
from jax import lax
from jax.experimental import pallas as pl
from jax.experimental.pallas import tpu as pltpu
from jax.sharding import PartitionSpec as P

H = 2048
D = 7168
COEF_A = 3.4445
COEF_B = -4.775
COEF_C = 2.0315
EPS = 1e-07
GAIN = 0.2 * math.sqrt(max(H, D))

Z, CORES, Y, X = 16, 2, 4, 4
NDP, NBLK = Z * CORES, Y * X
ROWS = H // NBLK
COLS = D // NDP
LINE = H // NDP
PACK = LINE + 8
PAIR = 2 * CORES * COLS
MESH = pl.DeviceIdType.MESH
F32 = jnp.float32
BF16 = jnp.bfloat16

G1 = COEF_A * COEF_A
G2 = 2 * COEF_A * COEF_B
G3 = 2 * COEF_A * COEF_C + COEF_B * COEF_B
G4 = 2 * COEF_B * COEF_C
G5 = COEF_C * COEF_C

TREE = {0: (3, 1), 3: (6, 4), 1: (2,), 6: (8, 7), 4: (5,)}


def split(v):
    hi = v.astype(BF16)
    return hi, (v - hi.astype(F32)).astype(BF16)


def mm(left, right):
    m = left.shape[0]
    lh, ll = split(left)
    rh, rl = split(right)
    both = jnp.dot(
        jnp.concatenate([lh, ll], axis=0),
        jnp.concatenate([rh, rl], axis=1),
        preferred_element_type=F32,
    )
    n = right.shape[1]
    return both[:m, :n] + (both[:m, n:] + (both[m:, :n] + both[m:, n:]))


def place():
    d = lax.axis_index("dp")
    b = lax.axis_index("blk")
    return d, b, d // CORES, d % CORES


def up(z, k):
    return lax.rem(z + (k + Z), Z)


def send(src, dst, ssem, rsem, to):
    pltpu.make_async_remote_copy(
        src_ref=src, dst_ref=dst, send_sem=ssem, recv_sem=rsem, device_id=to, device_id_type=MESH
    ).start()


def arrived(ref, sem):
    pltpu.make_async_copy(ref, ref, sem).wait()


def greet():
    d, b, z, c = place()
    bar = pltpu.get_barrier_semaphore()

    def in_plane(i, carry):
        pl.semaphore_signal(bar, inc=1, device_id=(d, lax.rem(b + i, NBLK)), device_id_type=MESH)
        return carry

    lax.fori_loop(1, NBLK, in_plane, 0)
    for k in (1, -1, 2, -2, 3, -3):
        pl.semaphore_signal(bar, inc=1, device_id=(up(z, k) * CORES + c, b), device_id_type=MESH)
    pl.semaphore_signal(bar, inc=1, device_id=(z * CORES + 1 - c, b), device_id_type=MESH)
    pl.semaphore_wait(bar, NBLK - 1 + 7)


class Ring:
    def __init__(self, buf, rows, near, far, cut, sub, sib_send, sib_recv, ring_send, ring_recv):
        self.buf, self.rows, self.near, self.far = buf, rows, near, far
        self.cut, self.sub = cut, sub
        self.sems = sib_send, sib_recv, ring_send, ring_recv
        self.d, self.b, self.z, self.c = place()

    def mine(self, zt, lo, n):
        return self.buf.at[pl.ds(pl.multiple_of((zt * CORES + self.c) * self.rows + lo, 8), n), :]

    def share(self, zt):
        start = pl.multiple_of((zt * CORES + 1 - self.c) * self.rows, 8)
        send(
            self.buf.at[pl.ds(start, self.rows), :],
            self.near.at[zt],
            self.sems[0],
            self.sems[1].at[zt],
            (self.z * CORES + 1 - self.c, self.b),
        )

    def shared(self, zt):
        arrived(self.near.at[zt], self.sems[1].at[zt])

    def pieces(self):
        h = self.rows // self.sub
        return [(q * h, h) for q in range(self.sub)]

    def first(self):
        zt = up(self.z, Z // 2)
        self.shared(zt)
        for q, (lo, n) in enumerate(self.cut):
            side = 0 if q < len(self.cut) // 2 else 1
            part = self.mine(zt, lo, n)
            part[...] = part[...] + self.near[zt, pl.ds(lo, n), :]
            self.push(part, side, 0, q, lo, n)

    def push(self, part, side, step, q, lo, n):
        slot = side * 8 + step
        send(
            part,
            self.far.at[slot, pl.ds(lo, n), :],
            self.sems[2],
            self.sems[3].at[slot * len(self.cut) + q],
            (up(self.z, 1 - 2 * side) * CORES + self.c, self.b),
        )

    def pull(self, side, step, q, lo, n):
        slot = side * 8 + step
        arrived(self.far.at[slot, pl.ds(lo, n), :], self.sems[3].at[slot * len(self.cut) + q])
        return self.far[slot, pl.ds(lo, n), :]

    def second(self):
        for side in (0, 1):
            zt = up(self.z, (1 - 2 * side) * 7)
            self.shared(zt)
        half = len(self.cut) // 2
        for side in (0, 1):
            zt = up(self.z, (1 - 2 * side) * 7)
            for q, (lo, n) in enumerate(self.cut):
                if (q < half) != (side == 0):
                    part = self.mine(zt, lo, n)
                    part[...] = part[...] + self.near[zt, pl.ds(lo, n), :]
                    if self.sub > 1:
                        self.push(part, side, 1, q, lo, n)
        for q, (lo, n) in enumerate(self.cut):
            side = 0 if q < half else 1
            zt = up(self.z, (1 - 2 * side) * 7)
            part = self.mine(zt, lo, n)
            got = self.pull(side, 0, q, lo, n)
            part[...] = part[...] + (self.near[zt, pl.ds(lo, n), :] + got)
            if self.sub > 1:
                self.push(part, side, 1, q, lo, n)
        if self.sub == 1:
            for side in (0, 1):
                zt = up(self.z, (1 - 2 * side) * 7)
                self.push(self.mine(zt, 0, self.rows), side, 1, 0, 0, self.rows)

    def rest(self):
        def step(s, carry):
            for side in (0, 1):
                self.shared(lax.rem(self.z + (1 - 2 * side) * (8 - s) + Z, Z))
            for q, (lo, n) in enumerate(self.pieces()):
                for side in (0, 1):
                    zt = lax.rem(self.z + (1 - 2 * side) * (8 - s) + Z, Z)
                    part = self.mine(zt, lo, n)
                    got = self.pull(side, s - 1, q, lo, n)
                    part[...] = part[...] + (self.near[zt, pl.ds(lo, n), :] + got)
                    self.push(part, side, s, q, lo, n)
            return carry

        lax.fori_loop(2, 8, step, 0)
        self.shared(self.z)

    def total(self, q, lo, n):
        own = self.mine(self.z, lo, n)[...] + self.near[self.z, pl.ds(lo, n), :]
        return own + (self.pull(0, 7, q, lo, n) + self.pull(1, 7, q, lo, n))

    def drain(self):
        arrived(self.near, self.sems[0])
        arrived(self.far.at[pl.ds(0, 15)], self.sems[2])


class Plane:
    def __init__(self, buf, ssem, rsem):
        self.buf, self.ssem, self.rsem = buf, ssem, rsem
        self.d, self.b, _, _ = place()

    def start(self, value):
        mine = self.buf.at[:, pl.ds(pl.multiple_of(self.b * 128, 128), 128)]
        mine[...] = value

        def one(i, carry):
            send(mine, mine, self.ssem, self.rsem, (self.d, lax.rem(self.b + i, NBLK)))
            return carry

        lax.fori_loop(1, NBLK, one, 0)

    def finish(self):
        arrived(self.buf.at[:, pl.ds(0, (NBLK - 1) * 128)], self.rsem)

    def drain(self):
        arrived(self.buf.at[:, pl.ds(0, (NBLK - 1) * 128)], self.ssem)


class Line:
    def __init__(self, buf, ssem, rsem, share_ssem, share_rsem):
        self.buf, self.ssem, self.rsem = buf, ssem, rsem
        self.share_sems = share_ssem, share_rsem
        self.d, self.b, self.z, self.c = place()

    def part(self, side, k, child):
        dd = up(self.z, -side * k) * CORES + self.c
        lo, n = 0, LINE
        if child == 8:
            n = LINE // 2
            lo = 0 if side > 0 else n
        return self.buf.at[pl.ds(pl.multiple_of(dd * LINE + lo, 8), n), :]

    def sem(self, side, k):
        return self.rsem.at[(0 if side > 0 else 8) + k - 1]

    def emit(self, k):
        for child in TREE.get(k, ()):
            for side in (1, -1):
                v = self.part(side, k, child)
                to = up(self.z, side * (child - k)) * CORES + self.c
                send(v, v, self.ssem, self.sem(side, child), (to, self.b))

    def share(self, dz):
        dd = up(self.z, dz) * CORES + self.c
        v = self.buf.at[pl.ds(pl.multiple_of(dd * LINE, 8), LINE), :]
        send(v, v, self.share_sems[0], self.share_sems[1], (self.z * CORES + 1 - self.c, self.b))

    def start(self, value):
        v = self.buf.at[pl.ds(pl.multiple_of(self.d * LINE, 8), LINE), :]
        v[...] = value
        self.emit(0)
        self.share(0)

    def take(self, k):
        for side in (1, -1):
            arrived(self.part(side, k, k), self.sem(side, k))
        self.emit(k)
        self.share(-k)
        if k != 8:
            self.share(k)

    def relay(self, stage):
        for k in ((3, 1), (6, 4, 2), (5, 7, 8))[stage]:
            self.take(k)

    def finish(self):
        arrived(self.buf.at[pl.ds(0, H // 2), :], self.share_sems[1])

    def drain(self):
        arrived(self.buf.at[pl.ds(0, 15 * LINE), :], self.ssem)
        arrived(self.buf.at[pl.ds(0, H // 2), :], self.share_sems[0])


def eye(rows, cols, row0, col0, value):
    r = lax.broadcasted_iota(jnp.int32, (rows, cols), 0) + row0
    c = lax.broadcasted_iota(jnp.int32, (rows, cols), 1) + col0
    return jnp.where(r == c, F32(value), F32(0))


def kernel(
    counts, partials, out, pt, sb, rv, ft, pg, sg, rg, zb, xb, yt,
    sib_s, sib_r, ring_s, ring_r, gsib_s, gsib_r, gring_s, gring_r,
    plane_s, plane_r, line_s, line_r, lshare_s, lshare_r,
):
    d, b, z, c = place()
    greet()

    weight = counts[0].astype(F32)
    scaled_eye = (eye(128, 128, 0, 0, 1.0) * weight).astype(BF16)
    ring = Ring(
        pt, COLS, sb, rv, [(q * 56, 56) for q in range(4)], 4, sib_s, sib_r, ring_s, ring_r
    )
    pair0 = up(z, Z // 2) // 2

    def turn(j):
        pair = lax.rem(pair0 + j + 8, 8)
        for t in range(7):
            at = pl.multiple_of(pair * PAIR + t * 128, 128)
            tile = partials[0, :, pl.ds(at, 128)]
            pt[pl.ds(at, 128), :] = lax.dot_general(
                scaled_eye, tile, (((1,), (1,)), ((), ())), preferred_element_type=F32
            )
        ring.share(pair * 2)
        ring.share(pair * 2 + 1)

    for j in (0, -1, 1):
        turn(j)
    ring.first()
    for j in (-2, 2, -3, 3, 4):
        turn(j)
    ring.second()
    ring.rest()
    field = jnp.concatenate([ring.total(q, q * 56, 56) for q in range(4)], axis=0)

    whole = Plane(ft, plane_s.at[7], plane_r.at[7])
    whole.start(field)
    whole.finish()

    fh, fl = split(ft[:, pl.ds(pl.multiple_of(b * 128, 128), 128)])
    right = jnp.concatenate([fh, fl], axis=1)

    def gram(i, sq):
        v = ft[:, pl.ds(pl.multiple_of(i * 128, 128), 128)]
        vh, vl = split(v)
        both = lax.dot_general(
            jnp.concatenate([vh, vl], axis=1), right, (((0,), (0,)), ((), ())), preferred_element_type=F32
        )
        res = both[:128, :128] + (both[:128, 128:] + (both[128:, :128] + both[128:, 128:]))
        at = pl.multiple_of(i * 2 * PACK, 8)
        pg[pl.ds(at, LINE), :] = res[:LINE]
        pg[pl.ds(pl.multiple_of(at + PACK, 8), LINE), :] = res[LINE:]
        return sq + jnp.sum(v * v, axis=0, keepdims=True)

    sq = lax.fori_loop(0, NBLK, gram, jnp.zeros((1, 128), F32))
    sq = jnp.broadcast_to(jnp.sum(sq, axis=1, keepdims=True), (8, 128))

    def put(i, carry):
        pg[pl.ds(pl.multiple_of(i * PACK + LINE, 8), 8), :] = sq
        return carry

    lax.fori_loop(0, NDP, put, 0)

    gr = Ring(pg, PACK, sg, rg, [(0, 40), (40, 32)], 1, gsib_s, gsib_r, gring_s, gring_r)

    def share(i, carry):
        gr.share(lax.rem(z + 8 + i, Z))
        return carry

    lax.fori_loop(0, Z, share, 0)
    gr.first()
    gr.second()
    gr.rest()
    packed = gr.total(0, 0, PACK)
    scale = jnp.sqrt(packed[LINE:LINE + 1, :]) + EPS
    inv = 1.0 / scale
    g = packed[:LINE] * (inv * inv)

    def line(i):
        return Line(zb.at[i], line_s.at[i], line_r.at[i], lshare_s.at[i], lshare_r.at[i])

    def plane(i):
        return Plane(xb.at[i], plane_s.at[i], plane_r.at[i])

    used = []

    def turn_field(g, base, between):
        zg, zs = line(base), line(base + 1)
        xg, xs, xw = plane(base * 3 // 2), plane(base * 3 // 2 + 1), plane(base * 3 // 2 + 2)
        used.extend([zg, zs, xg, xs, xw])
        zg.start(g)
        xg.start(g)
        for stage in range(3):
            zg.relay(stage)
        xg.finish()
        zg.finish()
        s = mm(xg.buf[...], zg.buf[...])
        zs.start(s)
        xs.start(s)
        zs.relay(0)
        xs.finish()
        t = mm(xs.buf[...], zg.buf[...])
        w = G3 * g + G4 * s + G5 * t
        xw.start(w)
        zs.relay(1)
        between(xg.buf, xs.buf)
        zs.relay(2)
        zs.finish()
        xw.finish()
        return G1 * g + G2 * s + mm(xw.buf[...], zs.buf[...])

    g = turn_field(g, 0, lambda xg, xs: None)

    zq = line(6)
    used.append(zq)

    def between(xg, xs):
        left = COEF_B * xg[...] + COEF_C * xs[...] + eye(LINE, H, d * LINE, 0, COEF_A)
        right = COEF_B * zb[0] + COEF_C * zb[1] + eye(H, 128, 0, b * 128, COEF_A)
        zq.start(mm(left, right))

    g = turn_field(g, 2, between)

    zg, zs = line(4), line(5)
    xg = plane(6)
    xy = Plane(yt, plane_s.at[8], plane_r.at[8])
    used.extend([zg, zs, xg, xy, whole, ring, gr])
    zq.relay(0)
    zg.start(g)
    xg.start(g)
    zq.relay(1)
    zg.relay(0)
    zq.relay(2)
    zq.finish()
    xy.start(mm(ft[...], zb[6]) * (inv * GAIN))
    zg.relay(1)
    zg.relay(2)
    xg.finish()
    zg.finish()
    zs.start(mm(xg.buf[...], zg.buf[...]))
    for stage in range(3):
        zs.relay(stage)
    zs.finish()
    xy.finish()
    last = COEF_B * zg.buf[...] + COEF_C * zs.buf[...] + eye(H, 128, 0, b * 128, COEF_A)
    out[...] = mm(yt[...], last)
    for one in used:
        one.drain()


def body(partials, counts):
    vmem = pltpu.VMEM
    dma = pltpu.SemaphoreType.DMA
    out = pl.pallas_call(
        kernel,
        name="newton_schulz",
        out_shape=jax.ShapeDtypeStruct((COLS, ROWS), F32),
        in_specs=[
            pl.BlockSpec(memory_space=pltpu.SMEM),
            pl.BlockSpec(memory_space=pltpu.VMEM),
        ],
        out_specs=pl.BlockSpec(memory_space=pltpu.VMEM),
        scratch_shapes=[
            vmem((D, 128), F32),
            vmem((Z, COLS, 128), F32),
            vmem((16, COLS, 128), F32),
            vmem((COLS, H), F32),
            vmem((NDP * PACK, 128), F32),
            vmem((Z, PACK, 128), F32),
            vmem((16, PACK, 128), F32),
            vmem((7, H, 128), F32),
            vmem((7, LINE, H), F32),
            vmem((COLS, H), F32),
            dma, dma((Z,)), dma, dma((64,)),
            dma, dma((Z,)), dma, dma((32,)),
            dma((9,)), dma((9,)),
            dma((7,)), dma((7, 16)), dma((7,)), dma((7,)),
        ],
        compiler_params=pltpu.CompilerParams(
            collective_id=0, has_side_effects=True, vmem_limit_bytes=56 * 2**20
        ),
    )(counts, partials)
    return out.T


def solution(mesh):
    placed = (P("dp", "blk", None), P("dp"))
    return jax.shard_map(
        body, mesh=mesh, in_specs=placed, out_specs=P("blk", "dp"), check_vma=False
    )
```

time: 1270 us -> 214 us (0.17)
  waiting for transfers between devices: 1110 us -> 0 us
  Pallas kernels: 0 us -> 212 us
  blocking collectives: 107 us -> 0 us
  matrix products: 33.4 us -> 0 us
  between operations: 14.9 us -> 0.66 us
    psum x3 -> x0, waiting for transfers between devices: 633 us -> none  [products(): gram = lax.psum(gram_part, 'dp')]
    all_gather x6 -> x0, waiting for transfers between devices: 360 us -> none  [the longest x3 182 us: products(): prod_whole = lax.all_gather(prod, 'blk', axis=0, tiled=True)]
    pallas_call x0 -> x1, Pallas kernels: none -> 212 us  [body(): pl.pallas_call(kernel, name='newton_schulz', out_shape=jax.ShapeDtypeStru...]
    reduce_scatter x1 -> x0, waiting for transfers between devices: 115 us -> none  [body(): field = lax.psum_scatter(weighted, 'dp', scatter_dimension=1, tiled=True)]
    psum x1 -> x0, blocking collectives: 107 us -> none  [body(): total_sq = lax.psum(jnp.sum(field * field), ('dp', 'blk'))]
    dot_general x9 -> x0, matrix products: 33.4 us -> none  [the longest x6 21.9 us: mult(): jnp.dot(left, right, precision=lax.Precision.HIGHEST, preferred_element_t...]
  transfers between devices with their start and end apart: 10 -> 0, of which waited for: 10 -> 0; matrix products, arithmetic and copies ran while one was open for 0% -> 0% of each run, Pallas kernels for 0% -> 0%
where the time goes in v1:
time: 214 us
  Pallas kernels  212 us (99%)
    pallas_call x1, Pallas kernels, body(): pl.pallas_call(kernel, name='newton_schulz', out_shape=jax.ShapeDtypeStru...  212 us

profile of v1, /device:TPU:1, one launch (start us, length us, event | category | flops | bytes accessed | tf_op | source)
XLA Modules:
  0.0 213.8 jit_solution(4611061050273848838)
XLA Ops:
  0.7 211.6 %newton_schulz.1 = f32[224,128]{1,0:T(8,128)} custom-call(s32[1]{0:T(128)S(6)} %copy.4.counts, bf16[1,128,7168]{2,1,0:T(8,128)(2,1)} %partials.1), custom_call_target="tpu_custom_call" | custom-call | tf_op jit(solution)/shard_map/newton_schulz/pallas_call | solution.py:429
  212.3 1.6 copy.5

commit v2 on v1

--- a/solution.py
+++ b/solution.py
@@ -21,18 +21,14 @@
 COLS = D // NDP
 LINE = H // NDP
 PACK = LINE + 8
+HALF = 40
 PAIR = 2 * CORES * COLS
 MESH = pl.DeviceIdType.MESH
 F32 = jnp.float32
 BF16 = jnp.bfloat16
 
-G1 = COEF_A * COEF_A
-G2 = 2 * COEF_A * COEF_B
-G3 = 2 * COEF_A * COEF_C + COEF_B * COEF_B
-G4 = 2 * COEF_B * COEF_C
-G5 = COEF_C * COEF_C
-
 TREE = {0: (3, 1), 3: (6, 4), 1: (2,), 6: (8, 7), 4: (5,)}
+PARENT = {child: k for k, children in TREE.items() for child in children}
 
 
 def split(v):
@@ -40,17 +36,17 @@
     return hi, (v - hi.astype(F32)).astype(BF16)
 
 
-def mm(left, right):
+def cut(right, halves):
+    hi, lo = split(right)
+    halves[:, :128] = hi
+    halves[:, 128:] = lo
+
+
+def mm(left, halves):
     m = left.shape[0]
     lh, ll = split(left)
-    rh, rl = split(right)
-    both = jnp.dot(
-        jnp.concatenate([lh, ll], axis=0),
-        jnp.concatenate([rh, rl], axis=1),
-        preferred_element_type=F32,
-    )
-    n = right.shape[1]
-    return both[:m, :n] + (both[:m, n:] + (both[m:, :n] + both[m:, n:]))
+    both = jnp.dot(jnp.concatenate([lh, ll], axis=0), halves[...], preferred_element_type=F32)
+    return both[:m, :128] + (both[:m, 128:] + (both[m:, :128] + both[m:, 128:]))
 
 
 def place():
@@ -85,7 +81,10 @@
     for k in (1, -1, 2, -2, 3, -3):
         pl.semaphore_signal(bar, inc=1, device_id=(up(z, k) * CORES + c, b), device_id_type=MESH)
     pl.semaphore_signal(bar, inc=1, device_id=(z * CORES + 1 - c, b), device_id_type=MESH)
-    pl.semaphore_wait(bar, NBLK - 1 + 7)
+
+
+def met():
+    pl.semaphore_wait(pltpu.get_barrier_semaphore(), NBLK - 1 + 7)
 
 
 class Ring:
@@ -190,6 +189,128 @@
         arrived(self.far.at[pl.ds(0, 15)], self.sems[2])
 
 
+class Fold:
+    def __init__(self, buf, near, far, sib_send, sib_recv, ssem, rsem):
+        self.buf, self.near, self.far = buf, near, far
+        self.sems = sib_send, sib_recv, ssem, rsem
+        self.d, self.b, self.z, self.c = place()
+
+    def share(self, zt):
+        start = pl.multiple_of((zt * CORES + 1 - self.c) * PACK, 8)
+        send(
+            self.buf.at[pl.ds(start, PACK), :],
+            self.near.at[zt],
+            self.sems[0],
+            self.sems[1].at[zt],
+            (self.z * CORES + 1 - self.c, self.b),
+        )
+
+    def span(self, side, k):
+        if k != 8:
+            return 0, PACK
+        return (0, HALF) if side > 0 else (HALF, PACK - HALF)
+
+    def landing(self, side, k):
+        slot = (0 if side > 0 else 8) + k - 1
+        lo, n = self.span(side, k)
+        return self.far.at[slot, pl.ds(lo, n), :], self.sems[3].at[slot]
+
+    def collect(self, zt, takes):
+        arrived(self.near.at[zt], self.sems[1].at[zt])
+        part = self.buf.at[pl.ds(pl.multiple_of((zt * CORES + self.c) * PACK, 8), PACK), :]
+        part[...] = part[...] + self.near[zt]
+        for side, child in takes:
+            ref, sem = self.landing(side, child)
+            lo, n = self.span(side, child)
+            arrived(ref, sem)
+            rows = part.at[pl.ds(lo, n), :]
+            rows[...] = rows[...] + ref[...]
+        return part
+
+    def push(self, part, side, k):
+        ref, sem = self.landing(side, k)
+        lo, n = self.span(side, k)
+        to = up(self.z, side * (k - PARENT[k])) * CORES + self.c
+        send(part.at[pl.ds(lo, n), :], ref, self.sems[2], sem, (to, self.b))
+
+    def run(self):
+        part = self.collect(up(self.z, 8), ())
+        for side in (1, -1):
+            self.push(part, side, 8)
+        for k in (7, 5, 2, 6, 4, 1, 3):
+            for side in (1, -1):
+                part = self.collect(up(self.z, side * k), [(side, n) for n in TREE.get(k, ())])
+                self.push(part, side, k)
+        return self.collect(self.z, [(side, n) for n in TREE[0] for side in (1, -1)])[...]
+
+    def drain(self):
+        arrived(self.near, self.sems[0])
+        arrived(self.far.at[pl.ds(0, 15)], self.sems[2])
+
+
+class Spread:
+    def __init__(self, buf, ssem, rsem):
+        self.buf, self.ssem, self.rsem = buf, ssem, rsem
+        self.d, self.b, _, self.c = place()
+
+    def block(self, u, v):
+        y, x = self.b // X, self.b % X
+        first = self.c == 0
+        xx = lax.rem(x + jnp.where(first, u, v) + X, X)
+        yy = lax.rem(y + jnp.where(first, v, u) + Y, Y)
+        return yy * X + xx
+
+    def part(self, u, v, half):
+        lo, n = {0: (0, COLS), 1: (0, COLS // 2), 2: (COLS // 2, COLS // 2)}[half]
+        return self.buf.at[pl.ds(lo, n), pl.ds(pl.multiple_of(self.block(u, v) * 128, 128), 128)]
+
+    def sem(self, u, v, half):
+        return self.rsem.at[((u + 1) * 4 + v + 1) * 2 + half // 2]
+
+    def send(self, u, v, half, axis, step):
+        to = (step, 0) if axis == 0 else (0, step)
+        seen = [u - to[0], v - to[1]]
+        seen = [2 if n == -2 else n for n in seen]
+        ref = self.part(u, v, half)
+        send(ref, ref, self.ssem, self.sem(*seen, half), (self.d, self.block(*to)))
+
+    def take(self, u, v, half=0):
+        arrived(self.part(u, v, half), self.sem(u, v, half))
+
+    def steps(self, value):
+        self.part(0, 0, 0)[...] = value
+        for axis in (0, 1):
+            for step in (1, -1):
+                self.send(0, 0, 0, axis, step)
+        yield [self.b]
+        for u, half in ((-1, 1), (1, 2)):
+            self.take(u, 0)
+            self.send(u, 0, half, 0, -u)
+            for step in (1, -1):
+                self.send(u, 0, 0, 1, step)
+        for v, half in ((-1, 1), (1, 2)):
+            self.take(0, v)
+            self.send(0, v, half, 1, -v)
+        yield [self.block(-1, 0), self.block(1, 0)]
+        for half in (1, 2):
+            self.take(2, 0, half)
+        for step in (1, -1):
+            self.send(2, 0, 0, 1, step)
+        yield [self.block(0, -1), self.block(0, 1), self.block(2, 0)]
+        for u in (-1, 1, 2):
+            for v, half in ((-1, 1), (1, 2)):
+                self.take(u, v)
+                self.send(u, v, half, 1, -v)
+            yield [self.block(u, -1), self.block(u, 1)]
+        for u in (0, -1, 1, 2):
+            for half in (1, 2):
+                self.take(u, 2, half)
+            yield [self.block(u, 2)]
+
+    def drain(self):
+        arrived(self.buf.at[:, pl.ds(0, (NBLK - 1) * 128)], self.ssem)
+
+
 class Plane:
     def __init__(self, buf, ssem, rsem):
         self.buf, self.ssem, self.rsem = buf, ssem, rsem
@@ -274,151 +395,148 @@
 
 
 def kernel(
-    counts, partials, out, pt, sb, rv, ft, pg, sg, rg, zb, xb, yt,
-    sib_s, sib_r, ring_s, ring_r, gsib_s, gsib_r, gring_s, gring_r,
+    counts, partials, out, pin, pt, sb, rv, ft, pg, sg, rg, zb, xb, xg0, yt, zc, zd,
+    in_s, sib_s, sib_r, ring_s, ring_r, field_s, field_r, gsib_s, gsib_r, fold_s, fold_r,
     plane_s, plane_r, line_s, line_r, lshare_s, lshare_r,
 ):
     d, b, z, c = place()
     greet()
+    pair0 = up(z, Z // 2) // 2
+
+    def load(j):
+        at = pl.multiple_of(lax.rem(pair0 + j + 8, 8) * PAIR, 128)
+        window = pl.ds(at, PAIR)
+        return pltpu.make_async_copy(partials.at[0, :, window], pin.at[:, window], in_s.at[j + 3])
+
+    turns = (0, -1, 1, -2, 2, -3, 3, 4)
+    for j in turns:
+        load(j).start()
 
     weight = counts[0].astype(F32)
     scaled_eye = (eye(128, 128, 0, 0, 1.0) * weight).astype(BF16)
-    ring = Ring(
-        pt, COLS, sb, rv, [(q * 56, 56) for q in range(4)], 4, sib_s, sib_r, ring_s, ring_r
-    )
-    pair0 = up(z, Z // 2) // 2
-
-    def turn(j):
+    for j in turns:
+        load(j).wait()
         pair = lax.rem(pair0 + j + 8, 8)
         for t in range(7):
             at = pl.multiple_of(pair * PAIR + t * 128, 128)
-            tile = partials[0, :, pl.ds(at, 128)]
             pt[pl.ds(at, 128), :] = lax.dot_general(
-                scaled_eye, tile, (((1,), (1,)), ((), ())), preferred_element_type=F32
+                scaled_eye, pin[:, pl.ds(at, 128)], (((1,), (1,)), ((), ())), preferred_element_type=F32
             )
+    met()
+    used = []
+    ring = Ring(
+        pt, COLS, sb, rv, [(q * 32, 32) for q in range(7)], 7, sib_s, sib_r, ring_s, ring_r
+    )
+    used.append(ring)
+    for j in turns:
+        pair = lax.rem(pair0 + j + 8, 8)
         ring.share(pair * 2)
         ring.share(pair * 2 + 1)
-
-    for j in (0, -1, 1):
-        turn(j)
     ring.first()
-    for j in (-2, 2, -3, 3, 4):
-        turn(j)
     ring.second()
     ring.rest()
-    field = jnp.concatenate([ring.total(q, q * 56, 56) for q in range(4)], axis=0)
-
-    whole = Plane(ft, plane_s.at[7], plane_r.at[7])
-    whole.start(field)
-    whole.finish()
-
-    fh, fl = split(ft[:, pl.ds(pl.multiple_of(b * 128, 128), 128)])
-    right = jnp.concatenate([fh, fl], axis=1)
-
-    def gram(i, sq):
-        v = ft[:, pl.ds(pl.multiple_of(i * 128, 128), 128)]
-        vh, vl = split(v)
-        both = lax.dot_general(
-            jnp.concatenate([vh, vl], axis=1), right, (((0,), (0,)), ((), ())), preferred_element_type=F32
-        )
+    field = jnp.concatenate([ring.total(q, lo, n) for q, (lo, n) in enumerate(ring.cut)], axis=0)
+
+    sq = jnp.sum(jnp.sum(field * field, axis=0, keepdims=True), axis=1, keepdims=True)
+    sq = jnp.broadcast_to(sq, (8, 128))
+
+    def put(i, carry):
+        pg[pl.ds(pl.multiple_of(i * PACK + LINE, 8), 8), :] = sq
+        return carry
+
+    fold = Fold(pg, sg, rg, gsib_s, gsib_r, fold_s, fold_r)
+    whole = Spread(ft, field_s.at[0], field_r.at[0])
+    used.extend([whole, fold])
+    right = jnp.concatenate(split(field), axis=1)
+
+    def gram(i):
+        v = jnp.concatenate(split(ft[:, pl.ds(pl.multiple_of(i * 128, 128), 128)]), axis=1)
+        both = lax.dot_general(v, right, (((0,), (0,)), ((), ())), preferred_element_type=F32)
         res = both[:128, :128] + (both[:128, 128:] + (both[128:, :128] + both[128:, 128:]))
         at = pl.multiple_of(i * 2 * PACK, 8)
         pg[pl.ds(at, LINE), :] = res[:LINE]
         pg[pl.ds(pl.multiple_of(at + PACK, 8), LINE), :] = res[LINE:]
-        return sq + jnp.sum(v * v, axis=0, keepdims=True)
-
-    sq = lax.fori_loop(0, NBLK, gram, jnp.zeros((1, 128), F32))
-    sq = jnp.broadcast_to(jnp.sum(sq, axis=1, keepdims=True), (8, 128))
-
-    def put(i, carry):
-        pg[pl.ds(pl.multiple_of(i * PACK + LINE, 8), 8), :] = sq
-        return carry
+        fold.share(i)
 
     lax.fori_loop(0, NDP, put, 0)
-
-    gr = Ring(pg, PACK, sg, rg, [(0, 40), (40, 32)], 1, gsib_s, gsib_r, gring_s, gring_r)
-
-    def share(i, carry):
-        gr.share(lax.rem(z + 8 + i, Z))
-        return carry
-
-    lax.fori_loop(0, Z, share, 0)
-    gr.first()
-    gr.second()
-    gr.rest()
-    packed = gr.total(0, 0, PACK)
-    scale = jnp.sqrt(packed[LINE:LINE + 1, :]) + EPS
-    inv = 1.0 / scale
-    g = packed[:LINE] * (inv * inv)
+    for blocks in whole.steps(field):
+        for i in blocks:
+            gram(i)
+    packed = fold.run()
 
     def line(i):
-        return Line(zb.at[i], line_s.at[i], line_r.at[i], lshare_s.at[i], lshare_r.at[i])
-
-    def plane(i):
-        return Plane(xb.at[i], plane_s.at[i], plane_r.at[i])
-
-    used = []
-
-    def turn_field(g, base, between):
-        zg, zs = line(base), line(base + 1)
-        xg, xs, xw = plane(base * 3 // 2), plane(base * 3 // 2 + 1), plane(base * 3 // 2 + 2)
-        used.extend([zg, zs, xg, xs, xw])
-        zg.start(g)
-        xg.start(g)
+        one = Line(zb.at[i], line_s.at[i], line_r.at[i], lshare_s.at[i], lshare_r.at[i])
+        used.append(one)
+        return one
+
+    def plane(i, buf):
+        one = Plane(buf, plane_s.at[i], plane_r.at[i])
+        used.append(one)
+        return one
+
+    def square(packed, zg, xg, beside=lambda stage: None):
+        zg.start(packed[:LINE])
+        xg.start(packed)
+        beside(0)
         for stage in range(3):
             zg.relay(stage)
+            beside(stage + 1)
         xg.finish()
+        inv = F32(1)
+        if packed.shape[0] > LINE:
+            tiles = xg.buf[LINE:LINE + 1, :]
+            total = sum(tiles[:, i * 128:(i + 1) * 128] for i in range(NBLK))
+            inv = 1.0 / (jnp.sqrt(total[0, 0]) + EPS)
+        left = xg.buf[:LINE, :] * (inv * inv)
         zg.finish()
-        s = mm(xg.buf[...], zg.buf[...])
-        zs.start(s)
-        xs.start(s)
-        zs.relay(0)
-        xs.finish()
-        t = mm(xs.buf[...], zg.buf[...])
-        w = G3 * g + G4 * s + G5 * t
-        xw.start(w)
-        zs.relay(1)
-        between(xg.buf, xs.buf)
-        zs.relay(2)
-        zs.finish()
-        xw.finish()
-        return G1 * g + G2 * s + mm(xw.buf[...], zs.buf[...])
-
-    g = turn_field(g, 0, lambda xg, xs: None)
-
-    zq = line(6)
-    used.append(zq)
-
-    def between(xg, xs):
-        left = COEF_B * xg[...] + COEF_C * xs[...] + eye(LINE, H, d * LINE, 0, COEF_A)
-        right = COEF_B * zb[0] + COEF_C * zb[1] + eye(H, 128, 0, b * 128, COEF_A)
-        zq.start(mm(left, right))
-
-    g = turn_field(g, 2, between)
-
-    zg, zs = line(4), line(5)
-    xg = plane(6)
-    xy = Plane(yt, plane_s.at[8], plane_r.at[8])
-    used.extend([zg, zs, xg, xy, whole, ring, gr])
-    zq.relay(0)
-    zg.start(g)
-    xg.start(g)
-    zq.relay(1)
-    zg.relay(0)
-    zq.relay(2)
-    zq.finish()
-    xy.start(mm(ft[...], zb[6]) * (inv * GAIN))
-    zg.relay(1)
-    zg.relay(2)
-    xg.finish()
-    zg.finish()
-    zs.start(mm(xg.buf[...], zg.buf[...]))
+        cut(zg.buf[...], zc)
+        g = packed[:LINE] * (inv * inv)
+        return inv, COEF_B * g + COEF_C * (mm(left, zc) * (inv * inv)) + eye(LINE, 128, d * LINE, b * 128, COEF_A)
+
+    def advance(packed, i, beside=lambda stage: None):
+        zg = line(2 * i)
+        inv, p = square(packed, zg, plane(3 * i, xg0 if i == 0 else xb.at[0]), beside)
+        zp, xp, xu = line(2 * i + 1), plane(3 * i + 1, xb.at[1 + 2 * i]), plane(3 * i + 2, xb.at[2 + 2 * i])
+        zp.start(p)
+        xp.start(p)
+        beside(4)
+        zp.relay(0)
+        xp.finish()
+        xu.start(mm(xp.buf[...], zc) * (inv * inv))
+        zp.relay(1)
+        zp.relay(2)
+        zp.finish()
+        cut(zp.buf[...], zd)
+        xu.finish()
+        return inv, mm(xu.buf[...], zd)
+
+    inv, g = advance(packed, 0)
+
+    def apply(i, value):
+        one = Spread(yt.at[i], field_s.at[i + 1], field_r.at[i + 1])
+        used.append(one)
+        moves = []
+
+        def beside(stage):
+            if stage == 0:
+                moves.append(one.steps(value()))
+            for _ in range((1, 1, 2, 2, 9)[stage]):
+                next(moves[0], None)
+
+        return beside
+
+    first = apply(0, lambda: mm(ft[...], zd))
+    _, g = advance(g, 1, first)
+    second = apply(1, lambda: mm(yt[0], zd) * (inv * GAIN))
+    _, p = square(g, line(4), plane(6, xb.at[5]), second)
+    zp = line(5)
+    zp.start(p)
+    second(4)
     for stage in range(3):
-        zs.relay(stage)
-    zs.finish()
-    xy.finish()
-    last = COEF_B * zg.buf[...] + COEF_C * zs.buf[...] + eye(H, 128, 0, b * 128, COEF_A)
-    out[...] = mm(yt[...], last)
+        zp.relay(stage)
+    zp.finish()
+    cut(zp.buf[...], zd)
+    out[...] = mm(yt[1], zd)
     for one in used:
         one.drain()
 
@@ -432,10 +550,11 @@
         out_shape=jax.ShapeDtypeStruct((COLS, ROWS), F32),
         in_specs=[
             pl.BlockSpec(memory_space=pltpu.SMEM),
-            pl.BlockSpec(memory_space=pltpu.VMEM),
+            pl.BlockSpec(memory_space=pl.ANY),
         ],
         out_specs=pl.BlockSpec(memory_space=pltpu.VMEM),
         scratch_shapes=[
+            vmem((ROWS, D), BF16),
             vmem((D, 128), F32),
             vmem((Z, COLS, 128), F32),
             vmem((16, COLS, 128), F32),
@@ -443,13 +562,17 @@
             vmem((NDP * PACK, 128), F32),
             vmem((Z, PACK, 128), F32),
             vmem((16, PACK, 128), F32),
-            vmem((7, H, 128), F32),
-            vmem((7, LINE, H), F32),
-            vmem((COLS, H), F32),
-            dma, dma((Z,)), dma, dma((64,)),
-            dma, dma((Z,)), dma, dma((32,)),
-            dma((9,)), dma((9,)),
-            dma((7,)), dma((7, 16)), dma((7,)), dma((7,)),
+            vmem((6, H, 128), F32),
+            vmem((6, LINE, H), F32),
+            vmem((PACK, H), F32),
+            vmem((2, COLS, H), F32),
+            vmem((H, 256), BF16),
+            vmem((H, 256), BF16),
+            dma((8,)), dma, dma((Z,)), dma, dma((112,)),
+            dma((3,)), dma((3, 32)),
+            dma, dma((Z,)), dma, dma((16,)),
+            dma((7,)), dma((7,)),
+            dma((6,)), dma((6, 16)), dma((6,)), dma((6,)),
         ],
         compiler_params=pltpu.CompilerParams(
             collective_id=0, has_side_effects=True, vmem_limit_bytes=56 * 2**20

time: 214 us -> 191 us (0.89)
  Pallas kernels: 212 us -> 188 us
    pallas_call x1, Pallas kernels: 212 us -> 188 us  [body(): pl.pallas_call(kernel, name='newton_schulz', out_shape=jax.ShapeDtypeStru...]
where the time goes in v2:
time: 191 us; the launch traced here: 190 us
  Pallas kernels  188 us (98%)
    pallas_call x1, Pallas kernels, body(): pl.pallas_call(kernel, name='newton_schulz', out_shape=jax.ShapeDtypeStru...  188 us

profile of v2, /device:TPU:1, one launch (start us, length us, event | category | flops | bytes accessed | tf_op | source)
XLA Modules:
  0.0 190.4 jit_solution(6504581534530034296)
XLA Ops:
  0.7 188.2 %newton_schulz.1 = f32[224,128]{1,0:T(8,128)} custom-call(s32[1]{0:T(128)S(6)} %copy.4.counts, bf16[1,128,7168]{2,1,0:T(8,128)(2,1)} %partials.1), custom_call_target="tpu_custom_call" | custom-call | tf_op jit(solution)/shard_map/newton_schulz/pallas_call | solution.py:547
  188.8 1.6 copy.5

commit v3 on v2

--- a/solution.py
+++ b/solution.py
@@ -21,6 +21,7 @@
 COLS = D // NDP
 LINE = H // NDP
 PACK = LINE + 8
+CUT = 128
 HALF = 40
 PAIR = 2 * CORES * COLS
 MESH = pl.DeviceIdType.MESH
@@ -28,6 +29,11 @@
 BF16 = jnp.bfloat16
 
 TREE = {0: (3, 1), 3: (6, 4), 1: (2,), 6: (8, 7), 4: (5,)}
+RELAY = {0: (5, 2, 1), 5: (8, 7, 6, 4), 2: (3,)}
+STAGES = ((2, 1, 5), (4, 6), (3, 7, 8))
+SETS = (((2, -2), (1, -1), (5, -5)), ((4, -4), (6, -6)), ((3, -3), (7, -7), (8, 0)))
+PARENT = {child: k for k, children in TREE.items() for child in children}
+NEAR = sorted(((u, v) for u in (-1, 0, 1, 2) for v in (-1, 0, 1, 2)), key=lambda o: abs(o[0]) + abs(o[1]))
 PARENT = {child: k for k, children in TREE.items() for child in children}
 
 
@@ -36,17 +42,25 @@
     return hi, (v - hi.astype(F32)).astype(BF16)
 
 
-def cut(right, halves):
-    hi, lo = split(right)
-    halves[:, :128] = hi
-    halves[:, 128:] = lo
+def stack(v, axis):
+    return jnp.concatenate(split(v), axis=axis)
+
+
+def merge(both):
+    m = both.shape[0] // 2
+    return both[:m, :128] + (both[:m, 128:] + (both[m:, :128] + both[m:, 128:]))
+
+
+def flat(buf):
+    return jnp.concatenate([buf[i] for i in range(NBLK)], axis=1)
+
+
+def dot(left, right):
+    return jnp.dot(left, right, preferred_element_type=F32)
 
 
 def mm(left, halves):
-    m = left.shape[0]
-    lh, ll = split(left)
-    both = jnp.dot(jnp.concatenate([lh, ll], axis=0), halves[...], preferred_element_type=F32)
-    return both[:m, :128] + (both[:m, 128:] + (both[m:, :128] + both[m:, 128:]))
+    return merge(dot(stack(left, 0), halves[...]))
 
 
 def place():
@@ -59,6 +73,10 @@
     return lax.rem(z + (k + Z), Z)
 
 
+def up4(i, k):
+    return lax.rem(i + (k + 4), 4)
+
+
 def send(src, dst, ssem, rsem, to):
     pltpu.make_async_remote_copy(
         src_ref=src, dst_ref=dst, send_sem=ssem, recv_sem=rsem, device_id=to, device_id_type=MESH
@@ -78,13 +96,13 @@
         return carry
 
     lax.fori_loop(1, NBLK, in_plane, 0)
-    for k in (1, -1, 2, -2, 3, -3):
+    for k in (1, -1, 2, -2, 3, -3, 5, -5):
         pl.semaphore_signal(bar, inc=1, device_id=(up(z, k) * CORES + c, b), device_id_type=MESH)
     pl.semaphore_signal(bar, inc=1, device_id=(z * CORES + 1 - c, b), device_id_type=MESH)
 
 
 def met():
-    pl.semaphore_wait(pltpu.get_barrier_semaphore(), NBLK - 1 + 7)
+    pl.semaphore_wait(pltpu.get_barrier_semaphore(), NBLK - 1 + 9)
 
 
 class Ring:
@@ -251,64 +269,75 @@
 class Spread:
     def __init__(self, buf, ssem, rsem):
         self.buf, self.ssem, self.rsem = buf, ssem, rsem
-        self.d, self.b, _, self.c = place()
-
-    def block(self, u, v):
-        y, x = self.b // X, self.b % X
-        first = self.c == 0
-        xx = lax.rem(x + jnp.where(first, u, v) + X, X)
-        yy = lax.rem(y + jnp.where(first, v, u) + Y, Y)
-        return yy * X + xx
-
-    def part(self, u, v, half):
-        lo, n = {0: (0, COLS), 1: (0, COLS // 2), 2: (COLS // 2, COLS // 2)}[half]
-        return self.buf.at[pl.ds(lo, n), pl.ds(pl.multiple_of(self.block(u, v) * 128, 128), 128)]
-
-    def sem(self, u, v, half):
-        return self.rsem.at[((u + 1) * 4 + v + 1) * 2 + half // 2]
-
-    def send(self, u, v, half, axis, step):
+        self.d, self.b, _, _ = place()
+
+    def block(self, h, u, v):
+        u, v = (u, v) if h == 0 else (v, u)
+        return up4(self.b // X, v) * X + up4(self.b % X, u)
+
+    def part(self, h, u, v, half):
+        lo, n = ((0, CUT), (CUT, COLS - CUT))[h]
+        if half:
+            lo, n = lo + (half - 1) * n // 2, n // 2
+        return self.buf.at[self.block(h, u, v), pl.ds(lo, n), :]
+
+    def sem(self, h, u, v, half):
+        if half == 2:
+            return self.rsem.at[h * 24 + 16 + (2 if v == 0 else u + 1 + (u > 0))]
+        return self.rsem.at[h * 24 + (u + 1) * 4 + v + 1]
+
+    def send(self, h, u, v, half, axis, step):
         to = (step, 0) if axis == 0 else (0, step)
-        seen = [u - to[0], v - to[1]]
-        seen = [2 if n == -2 else n for n in seen]
-        ref = self.part(u, v, half)
-        send(ref, ref, self.ssem, self.sem(*seen, half), (self.d, self.block(*to)))
-
-    def take(self, u, v, half=0):
-        arrived(self.part(u, v, half), self.sem(u, v, half))
-
-    def steps(self, value):
-        self.part(0, 0, 0)[...] = value
-        for axis in (0, 1):
+        seen = [2 if n == -2 else n for n in (u - to[0], v - to[1])]
+        ref = self.part(h, u, v, half)
+        send(ref, ref, self.ssem, self.sem(h, *seen, half), (self.d, self.block(h, *to)))
+
+    def take(self, h, u, v, half=0):
+        arrived(self.part(h, u, v, half), self.sem(h, u, v, half))
+
+    def moves(self, h, value):
+        self.part(h, 0, 0, 0)[...] = value()
+        for axis in (1, 0):
             for step in (1, -1):
-                self.send(0, 0, 0, axis, step)
-        yield [self.b]
+                self.send(h, 0, 0, 0, axis, step)
+        yield [(0, 0)]
         for u, half in ((-1, 1), (1, 2)):
-            self.take(u, 0)
-            self.send(u, 0, half, 0, -u)
+            self.take(h, u, 0)
+            self.send(h, u, 0, half, 0, -u)
             for step in (1, -1):
-                self.send(u, 0, 0, 1, step)
+                self.send(h, u, 0, 0, 1, step)
+        yield [(-1, 0), (1, 0)]
         for v, half in ((-1, 1), (1, 2)):
-            self.take(0, v)
-            self.send(0, v, half, 1, -v)
-        yield [self.block(-1, 0), self.block(1, 0)]
+            self.take(h, 0, v)
+            self.send(h, 0, v, half, 1, -v)
         for half in (1, 2):
-            self.take(2, 0, half)
+            self.take(h, 2, 0, half)
         for step in (1, -1):
-            self.send(2, 0, 0, 1, step)
-        yield [self.block(0, -1), self.block(0, 1), self.block(2, 0)]
+            self.send(h, 2, 0, 0, 1, step)
+        yield [(0, -1), (0, 1), (2, 0)]
         for u in (-1, 1, 2):
             for v, half in ((-1, 1), (1, 2)):
-                self.take(u, v)
-                self.send(u, v, half, 1, -v)
-            yield [self.block(u, -1), self.block(u, 1)]
+                self.take(h, u, v)
+                self.send(h, u, v, half, 1, -v)
+            yield [(u, -1), (u, 1)]
         for u in (0, -1, 1, 2):
             for half in (1, 2):
-                self.take(u, 2, half)
-            yield [self.block(u, 2)]
+                self.take(h, u, 2, half)
+            yield [(u, 2)]
+
+    def steps(self, value):
+        came = [set(), set()]
+        given = set()
+        halves = self.moves(0, lambda: value(0)), self.moves(1, lambda: value(1))
+        for first, second in zip(*halves):
+            came[0].update(first)
+            came[1].update((v, u) for u, v in second)
+            now = [o for o in NEAR if o in came[0] & came[1] - given]
+            given.update(now)
+            yield [self.block(0, *o) for o in now]
 
     def drain(self):
-        arrived(self.buf.at[:, pl.ds(0, (NBLK - 1) * 128)], self.ssem)
+        arrived(self.buf.at[pl.ds(0, NBLK - 1)], self.ssem)
 
 
 class Plane:
@@ -316,21 +345,42 @@
         self.buf, self.ssem, self.rsem = buf, ssem, rsem
         self.d, self.b, _, _ = place()
 
+    def block(self, u, v):
+        return up4(self.b // X, v) * X + up4(self.b % X, u)
+
+    def part(self, u, v):
+        return self.buf.at[self.block(u, v)]
+
+    def sem(self, u, v):
+        return self.rsem.at[(v + 1) * X + u + 1]
+
     def start(self, value):
-        mine = self.buf.at[:, pl.ds(pl.multiple_of(self.b * 128, 128), 128)]
+        mine = self.part(0, 0)
         mine[...] = value
-
-        def one(i, carry):
-            send(mine, mine, self.ssem, self.rsem, (self.d, lax.rem(self.b + i, NBLK)))
-            return carry
-
-        lax.fori_loop(1, NBLK, one, 0)
+        for u, v in NEAR[:0:-1]:
+            back = [2 if n == 2 else -n for n in (u, v)]
+            send(mine, mine, self.ssem, self.sem(*back), (self.d, self.block(u, v)))
+
+    def take(self, u, v):
+        if (u, v) != (0, 0):
+            arrived(self.part(u, v), self.sem(u, v))
+        return self.part(u, v)[...]
 
     def finish(self):
-        arrived(self.buf.at[:, pl.ds(0, (NBLK - 1) * 128)], self.rsem)
+        for u, v in NEAR[1:]:
+            arrived(self.part(u, v), self.sem(u, v))
+
+    def product(self, halves):
+        total = 0
+        for at in range(0, NBLK, 2):
+            pair = NEAR[at:at + 2]
+            left = jnp.concatenate([self.take(u, v) for u, v in pair], axis=1)
+            right = [halves[pl.ds(pl.multiple_of(self.block(u, v) * 128, 128), 128), :] for u, v in pair]
+            total += dot(stack(left, 0), jnp.concatenate(right, axis=0))
+        return merge(total)
 
     def drain(self):
-        arrived(self.buf.at[:, pl.ds(0, (NBLK - 1) * 128)], self.ssem)
+        arrived(self.buf.at[pl.ds(0, NBLK - 1)], self.ssem)
 
 
 class Line:
@@ -350,38 +400,47 @@
     def sem(self, side, k):
         return self.rsem.at[(0 if side > 0 else 8) + k - 1]
 
-    def emit(self, k):
-        for child in TREE.get(k, ()):
-            for side in (1, -1):
-                v = self.part(side, k, child)
-                to = up(self.z, side * (child - k)) * CORES + self.c
-                send(v, v, self.ssem, self.sem(side, child), (to, self.b))
+    def emit(self, k, side):
+        for child in RELAY.get(k, ()):
+            v = self.part(side, k, child)
+            to = up(self.z, side * (child - k)) * CORES + self.c
+            send(v, v, self.ssem, self.sem(side, child), (to, self.b))
 
     def share(self, dz):
         dd = up(self.z, dz) * CORES + self.c
         v = self.buf.at[pl.ds(pl.multiple_of(dd * LINE, 8), LINE), :]
-        send(v, v, self.share_sems[0], self.share_sems[1], (self.z * CORES + 1 - self.c, self.b))
+        stage = [any(dz in pair for pair in pairs) for pairs in SETS].index(True)
+        sem = self.share_sems[1].at[stage]
+        send(v, v, self.share_sems[0], sem, (self.z * CORES + 1 - self.c, self.b))
 
     def start(self, value):
         v = self.buf.at[pl.ds(pl.multiple_of(self.d * LINE, 8), LINE), :]
         v[...] = value
-        self.emit(0)
+        for side in (1, -1):
+            self.emit(0, side)
         self.share(0)
 
-    def take(self, k):
-        for side in (1, -1):
-            arrived(self.part(side, k, k), self.sem(side, k))
-        self.emit(k)
-        self.share(-k)
-        if k != 8:
+    def relay(self, stage):
+        for k in STAGES[stage]:
+            for side in (1, -1):
+                arrived(self.part(side, k, k), self.sem(side, k))
+                self.emit(k, side)
             self.share(k)
-
-    def relay(self, stage):
-        for k in ((3, 1), (6, 4, 2), (5, 7, 8))[stage]:
-            self.take(k)
-
-    def finish(self):
-        arrived(self.buf.at[pl.ds(0, H // 2), :], self.share_sems[1])
+            if k != 8:
+                self.share(-k)
+
+    def part_product(self, stage, halves, left=None):
+        pairs = SETS[stage]
+        arrived(self.buf.at[pl.ds(0, 2 * LINE * len(pairs)), :], self.share_sems[1].at[stage])
+        total = 0
+        for pair in pairs:
+            rows = [pl.ds(pl.multiple_of(up(self.z, k) * 128, 128), 128) for k in pair]
+            right = [stack(self.buf[r, :], 1) for r in rows]
+            for r, v in zip(rows, right):
+                halves[r, :] = v
+            if left is not None:
+                total += dot(jnp.concatenate([left[:, r] for r in rows], axis=1), jnp.concatenate(right, axis=0))
+        return total
 
     def drain(self):
         arrived(self.buf.at[pl.ds(0, 15 * LINE), :], self.ssem)
@@ -395,7 +454,7 @@
 
 
 def kernel(
-    counts, partials, out, pin, pt, sb, rv, ft, pg, sg, rg, zb, xb, xg0, yt, zc, zd,
+    counts, partials, out, pin, pt, sb, rv, ft, pg, sg, rg, zb, xb, xg0, yt, zc, zd, xc, yc,
     in_s, sib_s, sib_r, ring_s, ring_r, field_s, field_r, gsib_s, gsib_r, fold_s, fold_r,
     plane_s, plane_r, line_s, line_r, lshare_s, lshare_r,
 ):
@@ -435,7 +494,16 @@
     ring.first()
     ring.second()
     ring.rest()
-    field = jnp.concatenate([ring.total(q, lo, n) for q, (lo, n) in enumerate(ring.cut)], axis=0)
+
+    def summed(h):
+        pieces = ((0, 1, 2, 3), (4, 5, 6))[h]
+        return jnp.concatenate([ring.total(q, *ring.cut[q]) for q in pieces], axis=0)
+
+    whole = Spread(ft, field_s.at[0], field_r.at[0])
+    used.append(whole)
+    came = whole.steps(summed)
+    blocks = next(came)
+    field = ft[b]
 
     sq = jnp.sum(jnp.sum(field * field, axis=0, keepdims=True), axis=1, keepdims=True)
     sq = jnp.broadcast_to(sq, (8, 128))
@@ -445,23 +513,23 @@
         return carry
 
     fold = Fold(pg, sg, rg, gsib_s, gsib_r, fold_s, fold_r)
-    whole = Spread(ft, field_s.at[0], field_r.at[0])
-    used.extend([whole, fold])
-    right = jnp.concatenate(split(field), axis=1)
+    used.append(fold)
+    right = stack(field, 1)
 
     def gram(i):
-        v = jnp.concatenate(split(ft[:, pl.ds(pl.multiple_of(i * 128, 128), 128)]), axis=1)
+        v = stack(ft[i], 1)
         both = lax.dot_general(v, right, (((0,), (0,)), ((), ())), preferred_element_type=F32)
-        res = both[:128, :128] + (both[:128, 128:] + (both[128:, :128] + both[128:, 128:]))
+        res = merge(both)
         at = pl.multiple_of(i * 2 * PACK, 8)
         pg[pl.ds(at, LINE), :] = res[:LINE]
         pg[pl.ds(pl.multiple_of(at + PACK, 8), LINE), :] = res[LINE:]
         fold.share(i)
 
     lax.fori_loop(0, NDP, put, 0)
-    for blocks in whole.steps(field):
+    while blocks is not None:
         for i in blocks:
             gram(i)
+        blocks = next(came, None)
     packed = fold.run()
 
     def line(i):
@@ -478,20 +546,23 @@
         zg.start(packed[:LINE])
         xg.start(packed)
         beside(0)
-        for stage in range(3):
-            zg.relay(stage)
-            beside(stage + 1)
+        zg.relay(0)
+        beside(1)
+        zg.relay(1)
+        beside(2)
         xg.finish()
         inv = F32(1)
         if packed.shape[0] > LINE:
-            tiles = xg.buf[LINE:LINE + 1, :]
-            total = sum(tiles[:, i * 128:(i + 1) * 128] for i in range(NBLK))
+            total = sum(xg.buf[i, LINE:LINE + 1, :] for i in range(NBLK))
             inv = 1.0 / (jnp.sqrt(total[0, 0]) + EPS)
-        left = xg.buf[:LINE, :] * (inv * inv)
-        zg.finish()
-        cut(zg.buf[...], zc)
+        xc[...] = stack(flat(xg.buf)[:LINE] * (inv * inv), 0)
+        both = zg.part_product(0, zc, xc)
+        zg.relay(2)
+        beside(3)
+        both += zg.part_product(1, zc, xc)
+        both += zg.part_product(2, zc, xc)
         g = packed[:LINE] * (inv * inv)
-        return inv, COEF_B * g + COEF_C * (mm(left, zc) * (inv * inv)) + eye(LINE, 128, d * LINE, b * 128, COEF_A)
+        return inv, COEF_B * g + COEF_C * (merge(both) * (inv * inv)) + eye(LINE, 128, d * LINE, b * 128, COEF_A)
 
     def advance(packed, i, beside=lambda stage: None):
         zg = line(2 * i)
@@ -501,14 +572,13 @@
         xp.start(p)
         beside(4)
         zp.relay(0)
-        xp.finish()
-        xu.start(mm(xp.buf[...], zc) * (inv * inv))
+        xu.start(xp.product(zc) * (inv * inv))
         zp.relay(1)
+        zp.part_product(0, zd)
         zp.relay(2)
-        zp.finish()
-        cut(zp.buf[...], zd)
-        xu.finish()
-        return inv, mm(xu.buf[...], zd)
+        zp.part_product(1, zd)
+        zp.part_product(2, zd)
+        return inv, xu.product(zd)
 
     inv, g = advance(packed, 0)
 
@@ -519,24 +589,28 @@
 
         def beside(stage):
             if stage == 0:
-                moves.append(one.steps(value()))
+                v = value()
+                moves.append(one.steps(lambda h: v[:CUT] if h == 0 else v[CUT:]))
             for _ in range((1, 1, 2, 2, 9)[stage]):
                 next(moves[0], None)
 
         return beside
 
-    first = apply(0, lambda: mm(ft[...], zd))
+    first = apply(0, lambda: mm(flat(ft), zd))
     _, g = advance(g, 1, first)
-    second = apply(1, lambda: mm(yt[0], zd) * (inv * GAIN))
+    second = apply(1, lambda: mm(flat(yt.at[0]), zd) * (inv * GAIN))
     _, p = square(g, line(4), plane(6, xb.at[5]), second)
     zp = line(5)
     zp.start(p)
     second(4)
-    for stage in range(3):
-        zp.relay(stage)
-    zp.finish()
-    cut(zp.buf[...], zd)
-    out[...] = mm(yt[1], zd)
+    yc[...] = stack(flat(yt.at[1]), 0)
+    zp.relay(0)
+    zp.relay(1)
+    both = zp.part_product(0, zd, yc)
+    zp.relay(2)
+    both += zp.part_product(1, zd, yc)
+    both += zp.part_product(2, zd, yc)
+    out[...] = merge(both)
     for one in used:
         one.drain()
 
@@ -558,21 +632,23 @@
             vmem((D, 128), F32),
             vmem((Z, COLS, 128), F32),
             vmem((16, COLS, 128), F32),
-            vmem((COLS, H), F32),
+            vmem((NBLK, COLS, 128), F32),
             vmem((NDP * PACK, 128), F32),
             vmem((Z, PACK, 128), F32),
             vmem((16, PACK, 128), F32),
             vmem((6, H, 128), F32),
-            vmem((6, LINE, H), F32),
-            vmem((PACK, H), F32),
-            vmem((2, COLS, H), F32),
+            vmem((6, NBLK, LINE, 128), F32),
+            vmem((NBLK, PACK, 128), F32),
+            vmem((2, NBLK, COLS, 128), F32),
             vmem((H, 256), BF16),
             vmem((H, 256), BF16),
+            vmem((2 * LINE, H), BF16),
+            vmem((2 * COLS, H), BF16),
             dma((8,)), dma, dma((Z,)), dma, dma((112,)),
-            dma((3,)), dma((3, 32)),
+            dma((3,)), dma((3, 48)),
             dma, dma((Z,)), dma, dma((16,)),
-            dma((7,)), dma((7,)),
-            dma((6,)), dma((6, 16)), dma((6,)), dma((6,)),
+            dma((7,)), dma((7, 16)),
+            dma((6,)), dma((6, 16)), dma((6,)), dma((6, 3)),
         ],
         compiler_params=pltpu.CompilerParams(
             collective_id=0, has_side_effects=True, vmem_limit_bytes=56 * 2**20

time: 191 us -> 183 us (0.958)
  Pallas kernels: 188 us -> 181 us
    pallas_call x1, Pallas kernels: 188 us -> 181 us  [body(): pl.pallas_call(kernel, name='newton_schulz', out_shape=jax.ShapeDtypeStru...]
where the time goes in v3:
time: 183 us
  Pallas kernels  181 us (99%)
    pallas_call x1, Pallas kernels, body(): pl.pallas_call(kernel, name='newton_schulz', out_shape=jax.ShapeDtypeStru...  181 us

profile of v3, /device:TPU:1, one launch (start us, length us, event | category | flops | bytes accessed | tf_op | source)
XLA Modules:
  0.0 182.9 jit_solution(964249620719271548)
XLA Ops:
  0.7 180.7 %newton_schulz.1 = f32[224,128]{1,0:T(8,128)} custom-call(s32[1]{0:T(128)S(6)} %copy.4.counts, bf16[1,128,7168]{2,1,0:T(8,128)(2,1)} %partials.1), custom_call_target="tpu_custom_call" | custom-call | tf_op jit(solution)/shard_map/newton_schulz/pallas_call | solution.py:621
  181.3 1.6 copy.5
